TPU v7x, 128 devices: a whole 4x4x4 slice. The times are simulated.
128 devices in a mesh: block: 16 (over y, z_hi, core), day: 8 (over z_lo, x).
Axes of the slice: x: 4, y: 4, z: 4 (z_hi: 2, z_lo: 2; z = z_hi * 2 + z_lo), core: 2. Of those that a mesh axis runs over, the one named last changes fastest.
Arguments:
- spectra: bfloat16 [2, 128, 1536, 2048], P(None, None, 'day', 'block'), may hold values from -2000 to 2000
- valid: int32 [1536, 16], P('day', 'block'), may hold values from 0 to 1, as said below
Outputs:
- stacked: float32 [2, 128, 2, 2048, 128], P(None, 'day', None, 'block')
Inputs may be any that keep to these rules, and one draw needn't show every extreme that they name: `valid`: window 0 of every day is usable for every block.
All inputs are finite; a program needn't handle non-finite values.
Results may differ from a plain program's by a relative error of at most 0.015.
Values may be sent and summed in bfloat16 or wider, within the bound.
A program may use at most 256 MiB of HBM per device.

v0:
```python
import jax
import jax.numpy as jnp
from jax import lax
from jax.sharding import PartitionSpec as P

ROUNDS = 2


EPSILON = 1e-06


def swapped(block, axis, distance):
    count = lax.axis_size(axis)
    route = []
    for low in range(count):
        high = low | 1 << distance
        if high != low and high < count:
            route += [(low, high), (high, low)]
    return lax.ppermute(block, axis, route)


def whiten(spectra, valid_cells):
    values = spectra.astype(jnp.float32)
    power = jnp.mean(values[0] * values[0] + values[1] * values[1], axis=0)
    scaled = values / jnp.sqrt(power + EPSILON)
    return (scaled * valid_cells.astype(jnp.float32)).astype(jnp.bfloat16)


def cross_terms(first, second):
    left = jnp.concatenate((first[0], first[1]), axis=-1)
    right = jnp.concatenate((second[0], second[1]), axis=-1)
    grams = jnp.einsum("fdwc,fdwe->dfce", left, right, preferred_element_type=jnp.float32)
    width = first.shape[-1]
    real_part = grams[:, :, :width, :width] + grams[:, :, width:, width:]
    imag_part = grams[:, :, :width, width:] - grams[:, :, width:, :width]
    return jnp.stack((real_part, imag_part), axis=2)


def per_device(spectra, valid):
    whitened = whiten(spectra, valid)
    marks = valid[:, 0].astype(jnp.bfloat16)
    block_total = lax.axis_size("block")
    day_total = lax.axis_size("day")
    top_bit = block_total.bit_length() - 1
    freq_local = spectra.shape[1] // day_total
    results = []
    for round_index in range(ROUNDS):
        bit_number = top_bit - 1 - round_index
        partner, partner_marks = swapped((whitened, marks), "block", bit_number)
        correlation = jnp.sum(marks.astype(jnp.float32) * partner_marks.astype(jnp.float32))
        shared = lax.psum(correlation, "day")
        divisor = jnp.sqrt(shared)

        def term_rows(start, count, mine=whitened, theirs=partner):
            return cross_terms(mine[:, :, None], theirs[:, :, None])[0]

        summed = lax.psum_scatter(
            term_rows(jnp.int32(0), freq_local * lax.axis_size("day")).astype(jnp.bfloat16),
            "day",
            scatter_dimension=0,
            tiled=True,
        ).astype(jnp.float32)
        results.append(summed / divisor)
    return jnp.stack(results)


def solution(mesh):
    return jax.shard_map(
        per_device,
        mesh=mesh,
        in_specs=(P(None, None, "day", "block"), P("day", "block")),
        out_specs=P(None, "day", None, "block", None),
        check_vma=False,
    )
```

profile of v0, /device:TPU:0, one launch (start us, length us, event | category | flops | bytes accessed | tf_op | source)
XLA Modules:
  0.0 828.6 jit_solution(15214503547830136268)
XLA Ops:
  6.5 0.0 reduce-scatter.9.cloned.1.call-start
  6.5 7.2 convert_element_type.39
  13.7 0.0 copy-start.1
  13.7 2.0 fusion.1
  15.8 0.0 copy-done.1
  15.8 8.3 multiply_convert_fusion
  24.0 0.0 copy-start
  24.1 3.4 collective-permute-start
  27.4 6.2 slice_bitcast_fusion.5
  33.6 0.0 copy-done
  33.6 264.2 %collective-permute-done = bf16[2,128,192,128]{3,2,1,0:T(8,128)(2,1)S(1)} collective-permute-done((bf16[2,128,192,128]{3,2,1,0:T(8,128)(2,1)S(1)}, bf16[2,128,192,128]{3,2,1,0:T(8,128)(2,1)S(1)}, u32[]{:S(2)}, u32[]{:S(2)}) %collective-permute-start) | collective-permute-done | bytes 12582944 | tf_op jit(solution)/shard_map/ppermute | solution.py:19
  297.7 6.2 slice_bitcast_fusion.3
  303.9 20.2 %convolution_bitcast_fusion.1 = f32[1,128,256,256]{3,2,1,0:T(8,128)} fusion(bf16[128,1,192,128]{3,2,0,1:T(8,128)(2,1)} %get-tuple-element.14, bf16[128,1,192,128]{3,2,0,1:T(8,128)(2,1)} %get-tuple-element.13, bf16[128,1,192,128]{3,2,0,1:T(8,128)(2,1)} %get-tuple-element.16, bf16[128,1,192,128]{3,2,0,1:T(8,128)(2,1)} %get-tuple-element.15), kind=kOutput, calls=%fused_computation.2 | convolution fusion | flops 3271557120 | bytes 58720256 | tf_op jit(solution)/shard_map/fdwc,fdwe->dfce/dot_general | solution.py:32
  324.2 15.2 %fusion.10 = (bf16[1,128,1,128,128]{4,3,1,2,0:T(8,128)(2,1)S(1)}, bf16[1,128,1,128,128]{4,3,1,2,0:T(8,128)(2,1)}) fusion(f32[1,128,256,256]{3,2,1,0:T(8,128)} %convolution_bitcast_fusion.1), kind=kLoop, calls=%fused_computation.32 | loop fusion | flops 8388608 | bytes 41943040 | tf_op jit(solution)/shard_map/stack | solution.py:36
  339.4 6.2 maximum_bitcast_fusion.5
  345.6 10.3 %copy.5 = bf16[128,2,128,128]{3,2,1,0:T(8,128)(2,1)} copy(bf16[128,2,128,128]{3,2,0,1:T(8,128)(2,1)} %maximum_bitcast_fusion.5) | data formatting | bytes 16777216
  355.9 13.7 %copy.18 = bf16[16,8,256,128]{3,1,2,0:T(8,128)(2,1)} copy(bf16[16,8,256,128]{3,2,1,0:T(8,128)(2,1)} %bitcast.67) | data formatting | bytes 16777216
  369.6 0.0 reduce-scatter.9.cloned.1.call-update
  369.7 0.0 reduce-scatter.11.cloned.1.call-start
  369.7 1.7 collective-permute-start.2
  371.4 269.8 %collective-permute-done.2 = bf16[2,128,192,128]{3,2,1,0:T(8,128)(2,1)S(1)} collective-permute-done((bf16[2,128,192,128]{3,2,1,0:T(8,128)(2,1)}, bf16[2,128,192,128]{3,2,1,0:T(8,128)(2,1)S(1)}, u32[]{:S(2)}, u32[]{:S(2)}) %collective-permute-start.2) | collective-permute-done | bytes 12582944 | tf_op jit(solution)/shard_map/ppermute | solution.py:19
  641.3 6.2 slice_bitcast_fusion.1
  647.5 20.2 %convolution_bitcast_fusion = f32[1,128,256,256]{3,2,1,0:T(8,128)} fusion(bf16[128,1,192,128]{3,2,0,1:T(8,128)(2,1)} %get-tuple-element.18, bf16[128,1,192,128]{3,2,0,1:T(8,128)(2,1)} %get-tuple-element.17, bf16[128,1,192,128]{3,2,0,1:T(8,128)(2,1)} %get-tuple-element.16, bf16[128,1,192,128]{3,2,0,1:T(8,128)(2,1)} %get-tuple-element.15), kind=kOutput, calls=%fused_computation.1 | convolution fusion | flops 3271557120 | bytes 58720256 | tf_op jit(solution)/shard_map/fdwc,fdwe->dfce/dot_general | solution.py:32
  667.7 23.5 %fusion.12 = (bf16[1,128,1,128,128]{4,3,1,2,0:T(8,128)(2,1)S(1)}, bf16[1,128,1,128,128]{4,3,1,2,0:T(8,128)(2,1)}) fusion(f32[1,128,256,256]{3,2,1,0:T(8,128)} %convolution_bitcast_fusion), kind=kLoop, calls=%fused_computation.34 | loop fusion | flops 8388608 | bytes 41943040 | tf_op jit(solution)/shard_map/stack | solution.py:36
  691.3 6.2 maximum_bitcast_fusion.6
  697.4 10.3 %copy.7 = bf16[128,2,128,128]{3,2,1,0:T(8,128)(2,1)} copy(bf16[128,2,128,128]{3,2,0,1:T(8,128)(2,1)} %maximum_bitcast_fusion.6) | data formatting | bytes 16777216
  707.8 13.7 %copy.17 = bf16[16,8,256,128]{3,1,2,0:T(8,128)(2,1)} copy(bf16[16,8,256,128]{3,2,1,0:T(8,128)(2,1)} %bitcast.68) | data formatting | bytes 16777216
  721.4 0.0 reduce-scatter.11.cloned.1.call-update
  721.5 3.3 collective-permute-start.1
  724.8 0.7 collective-permute-start.3
  725.4 1.2 collective-permute-done.1
  726.6 1.7 collective-permute-done.3
  728.3 0.7 fusion.14
  729.0 21.2 %all-reduce = (f32[]{:T(128)}, f32[]{:T(128)}) all-reduce(f32[]{:T(128)} %get-tuple-element.6, f32[]{:T(128)} %get-tuple-element.5), channel_id=1, replica_groups=mesh['block'=16,'day'=8] {'day'}, use_global_device_ids=true, to_apply=%region_6.0 | all-reduce | flops 2 | bytes 16 | tf_op jit(solution)/shard_map/psum | solution.py:51
  751.5 0.0 reduce-scatter.9.cloned.1.call-done
  751.6 1.4 copy.10
  753.0 64.0 %reduce-scatter.11.cloned.1.call-done = bf16[16,32768]{1,0:T(8,128)(2,1)} async-done(((bf16[128,32768]{1,0:T(8,128)(2,1)}), bf16[16,32768]{1,0:T(8,128)(2,1)}) %reduce-scatter.11.cloned.1.call-update) | async-done | bytes 1048592
  817.0 1.4 copy.12
  818.4 0.6 divide_bitcast_fusion
  819.0 0.5 pad_maximum_fusion
  819.5 2.3 copy.4
  (3 shorter events, 0.1 us)
Async XLA Ops:
  6.5 745.0 %reduce-scatter.9.cloned.1.call-start = ((), (), s32[]{:S(2)}) async-start(), calls=%async_computation.2 | async-start | bytes 9437184
  13.7 2.0 copy-start.1
  24.0 9.5 %copy-start = (bf16[2,128,192,128]{3,2,1,0:T(8,128)(2,1)}, bf16[2,128,192,128]{3,2,1,0:T(8,128)(2,1)S(1)}, u32[]{:S(2)}) copy-start(bf16[2,128,192,128]{3,2,1,0:T(8,128)(2,1)S(1)} %multiply_convert_fusion) | copy-start | bytes 37748740
  24.1 273.7 %collective-permute-start = (bf16[2,128,192,128]{3,2,1,0:T(8,128)(2,1)S(1)}, bf16[2,128,192,128]{3,2,1,0:T(8,128)(2,1)S(1)}, u32[]{:S(2)}, u32[]{:S(2)}) collective-permute-start(bf16[2,128,192,128]{3,2,1,0:T(8,128)(2,1)S(1)} %multiply_convert_fusion), channel_id=1, source_target_pairs={{0,64},{64,0},{8,72},{72,8},{16,80},{80,16},{24,88},{88,24},{32,96... | collective-permute-start | bytes 37748744 | tf_op jit(solution)/shard_map/ppermute | solution.py:19
  369.7 447.3 %reduce-scatter.11.cloned.1.call-start = ((), (), s32[]{:S(2)}) async-start(), calls=%async_computation.3 | async-start | bytes 9437184
  369.7 271.5 %collective-permute-start.2 = (bf16[2,128,192,128]{3,2,1,0:T(8,128)(2,1)}, bf16[2,128,192,128]{3,2,1,0:T(8,128)(2,1)S(1)}, u32[]{:S(2)}, u32[]{:S(2)}) collective-permute-start(bf16[2,128,192,128]{3,2,1,0:T(8,128)(2,1)} %copy-done), channel_id=1, source_target_pairs={{0,32},{32,0},{8,40},{40,8},{16,48},{48,16},{24,56},{56,24},{64,96... | collective-permute-start | bytes 37748744 | tf_op jit(solution)/shard_map/ppermute | solution.py:19
  721.5 5.1 collective-permute-start.1
  724.8 3.5 collective-permute-start.3
Sparse Core Ops, SparseCore 0:
  369.8 95.1 reduce-scatter.8
  721.6 95.3 reduce-scatter.10
where the time goes:
time: 836 us; the launch traced here: 829 us
  waiting for transfers between devices  601 us (72%)
  local copies, waits for them, and re-layouts  71.8 us (9%)
  other arithmetic  70.2 us (8%)
  matrix products  40.5 us (5%)
  blocking collectives  21.2 us (3%)
  between operations  14.9 us (2%)
  starting transfers between devices  9.07 us (1%)
    ppermute x4, waiting for transfers between devices, swapped(): return lax.ppermute(block, axis, route)  537 us
    unnamed x4, waiting for transfers between devices  64 us
    unnamed x10, local copies, waits for them, and re-layouts  50.9 us
    dot_general x2, matrix products, cross_terms(): jnp.einsum('fdwc,fdwe->dfce', left, right, preferred_element_type=jnp.flo...  40.5 us
    another operation x2, other arithmetic, cross_terms(): return jnp.stack((real_part, imag_part), axis=2)  38.7 us
    psum x1, blocking collectives, per_device(): shared = lax.psum(correlation, 'day')  21.2 us
  transfers between devices with their start and end apart: 6, of which 5 were waited for; matrix products, arithmetic and copies ran while one was open for 11% of the time, Pallas kernels for 0%

commit v1 on v0

v1 whole, which is shorter than its diff:
```python
import functools

import jax
import jax.numpy as jnp
from jax import lax
from jax.experimental import pallas as pl
from jax.experimental.pallas import tpu as pltpu
from jax.sharding import PartitionSpec as P

EPSILON = 1e-06
RING = 4
MESH = pl.DeviceIdType.MESH


def kernel(
    sizes, spectra, marks, out,
    own, taken, scale, scales_in, partial, partials_in, back, back_in, result, counts, counts_in, inverse,
    own_sem, row_send, row_recv, scale_send, scale_recv, count_send, count_recv,
    part_send, part_recv, back_send, back_recv, out_sem,
):
    days, steps, windows, width = sizes
    f32, bf16 = jnp.float32, jnp.bfloat16
    block, day = lax.axis_index("block"), lax.axis_index("day")
    rest_total = lax.axis_size("block") // RING
    row, rest = block // rest_total, block % rest_total
    row_q = row + 1 - 2 * (row % 2)
    row_r = RING - 1 - row
    peers = (row_q * rest_total + rest, row_r * rest_total + rest)
    mine = ((row + 1) // 2) % 2
    other = 1 - mine

    def owner(offset):
        return (day + offset) % days

    def row_copy(side, step):
        half = other if side == 0 else mine
        return pltpu.make_async_remote_copy(
            src_ref=spectra.at[:, :, half, step],
            dst_ref=taken.at[side, step],
            send_sem=row_send.at[side, step],
            recv_sem=row_recv.at[side, step],
            device_id={"block": peers[side]},
            device_id_type=MESH,
        )

    def scale_copy(side):
        return pltpu.make_async_remote_copy(
            src_ref=scale,
            dst_ref=scales_in.at[side],
            send_sem=scale_send.at[side],
            recv_sem=scale_recv.at[side],
            device_id={"block": peers[side]},
            device_id_type=MESH,
        )

    def count_copy(offset):
        return pltpu.make_async_remote_copy(
            src_ref=counts,
            dst_ref=counts_in.at[offset],
            send_sem=count_send.at[offset],
            recv_sem=count_recv.at[offset],
            device_id={"day": owner(offset)},
            device_id_type=MESH,
        )

    def part_copy(step, offset):
        return pltpu.make_async_remote_copy(
            src_ref=partial.at[step, offset],
            dst_ref=partials_in.at[step, offset],
            send_sem=part_send.at[step, offset],
            recv_sem=part_recv.at[step, offset],
            device_id={"day": owner(offset)},
            device_id_type=MESH,
        )

    def back_copy(side, step):
        part = pl.ds(0, 4) if side == 0 else pl.ds(4, 2)
        return pltpu.make_async_remote_copy(
            src_ref=back.at[step, part],
            dst_ref=back_in.at[step, part],
            send_sem=back_send.at[side, step],
            recv_sem=back_recv.at[side, step],
            device_id={"block": peers[side]},
            device_id_type=MESH,
        )

    def own_copy(index):
        return pltpu.make_async_copy(spectra.at[:, index], own.at[:, index], own_sem.at[index])

    def out_copy(kind, step):
        if kind == 0:
            return pltpu.make_async_copy(result.at[1, mine, step], out.at[1, mine, step], out_sem.at[0, step])
        if kind == 1:
            return pltpu.make_async_copy(result.at[0, mine, step], out.at[0, mine, step], out_sem.at[1, step])
        return pltpu.make_async_copy(result.at[:, other, step], out.at[:, other, step], out_sem.at[2, step])

    for index in range(days):
        own_copy(index).start()

    barrier = pltpu.get_barrier_semaphore()
    for side in range(2):
        pl.semaphore_signal(barrier, inc=1, device_id={"block": peers[side]}, device_id_type=MESH)
    for offset in range(1, days):
        pl.semaphore_signal(barrier, inc=1, device_id={"day": owner(offset)}, device_id_type=MESH)
    pl.semaphore_wait(barrier, days + 1)

    for side in range(2):
        row_copy(side, 0).start()

    tile = 48 if windows % 48 == 0 else 16
    scale[...] = jnp.zeros_like(scale)

    @pl.loop(0, days)
    def _(index):
        own_copy(index).wait()

        @pl.loop(0, windows // tile)
        def _(piece):
            rows = pl.ds(pl.multiple_of(piece * tile, tile), tile)
            total = scale[rows, :]
            for half in range(2):
                for step in range(steps):
                    for k in range(2):
                        value = own[k, index, half, step, rows, :].astype(f32)
                        total = total + value * value
            scale[rows, :] = total

    bins = days * 2 * steps
    scale[...] = lax.rsqrt(scale[...] * (1.0 / bins) + EPSILON) * marks[...]
    for side in range(2):
        scale_copy(side).start()

    def whiten(value, factor):
        return (value.astype(f32) * factor).astype(bf16)

    def cross(step):
        @pl.loop(1, days + 1)
        def _(turn):
            offset = turn % days
            index = owner(offset)
            parts = []
            for k in range(2):
                parts.append((
                    whiten(taken[0, step, k, index], scales_in[0]),
                    whiten(taken[1, step, k, index], scales_in[1]),
                    whiten(own[k, index, mine, step], scale[...]),
                ))
            (q_re, r_re, s_re), (q_im, r_im, s_im) = parts
            top = jnp.concatenate((r_re, r_im, s_re, s_im), axis=1)
            low = jnp.concatenate((r_im, -r_re, s_im, -s_re), axis=1)
            dims = (((0,), (0,)), ((), ()))
            gram = lax.dot_general(q_re, top, dims, preferred_element_type=f32)
            gram = gram + lax.dot_general(q_im, low, dims, preferred_element_type=f32)
            for part in range(4):
                partial[step, offset, part] = gram[:, part * width:(part + 1) * width].astype(bf16)

            @pl.when(offset != 0)
            def _():
                part_copy(step, offset).start()

    def reduce(step):
        @pl.loop(1, days)
        def _(offset):
            part_copy(step, offset).wait_recv()

        def total(part):
            value = partial[step, 0, part].astype(f32)
            for offset in range(1, days):
                value = value + partials_in[step, offset, part].astype(f32)
            return value * inverse[pl.ds(part // 2, 1), :]

        re0, im0, re1, im1 = total(0), total(1), total(2), total(3)
        back[step, 0] = re0.astype(bf16)
        back[step, 1] = im0.astype(bf16)
        back[step, 2] = re1.astype(bf16)
        back[step, 3] = im1.astype(bf16)
        back_copy(0, step).start()
        back[step, 4] = re0.T.astype(bf16)
        back[step, 5] = (-im0.T).astype(bf16)
        back_copy(1, step).start()
        result[1, mine, step, 0] = re1.T
        result[1, mine, step, 1] = -im1.T
        out_copy(0, step).start()

    def finish(step):
        back_copy(1, step).wait_recv()
        result[0, mine, step] = back_in[step, pl.ds(4, 2)].astype(f32)
        out_copy(1, step).start()
        back_copy(0, step).wait_recv()
        result[0, other, step] = back_in[step, pl.ds(0, 2)].astype(f32)
        result[1, other, step] = back_in[step, pl.ds(2, 2)].astype(f32)
        out_copy(2, step).start()

    @pl.loop(0, steps + 2)
    def _(turn):
        @pl.when(turn < steps)
        def _():
            @pl.when(turn >= 1)
            def _():
                for side in range(2):
                    row_copy(side, turn - 1).wait_send()

            @pl.when(turn + 1 < steps)
            def _():
                for side in range(2):
                    row_copy(side, turn + 1).start()

            @pl.when(turn == 0)
            def _():
                for side in range(2):
                    scale_copy(side).wait_recv()
                seen_q = jnp.where(scales_in[0] > 0, 1.0, 0.0)
                seen_r = jnp.where(scales_in[1] > 0, 1.0, 0.0)
                first = jnp.sum(seen_q * seen_r, axis=0, keepdims=True)
                second = jnp.sum(seen_q * marks[...], axis=0, keepdims=True)
                counts[...] = jnp.concatenate((first, second) * 4, axis=0)

                @pl.loop(1, days)
                def _(offset):
                    count_copy(offset).start()

            for side in range(2):
                row_copy(side, turn).wait_recv()
            cross(turn)

        @pl.when(turn == 1)
        def _():
            value = counts[...]
            for offset in range(1, days):
                count_copy(offset).wait_recv()
                value = value + counts_in[offset]
            inverse[...] = lax.rsqrt(value)

        @pl.when(jnp.logical_and(turn >= 1, turn < steps + 1))
        def _():
            reduce(turn - 1)

        @pl.when(turn >= 2)
        def _():
            finish(turn - 2)

    for side in range(2):
        row_copy(side, steps - 1).wait_send()
        scale_copy(side).wait_send()

    @pl.loop(1, days)
    def _(offset):
        count_copy(offset).wait_send()

    @pl.loop(0, steps)
    def _(step):
        @pl.loop(1, days)
        def _(offset):
            part_copy(step, offset).wait_send()

        for side in range(2):
            back_copy(side, step).wait_send()
        for kind in range(3):
            out_copy(kind, step).wait()


def per_device(spectra, valid):
    days = lax.axis_size("day")
    _, bins, windows, width = spectra.shape
    steps = bins // days // 2
    f32, bf16 = jnp.float32, jnp.bfloat16
    marks = jnp.broadcast_to(valid.astype(f32), (windows, width))
    dma = pltpu.SemaphoreType.DMA
    stacked = pl.pallas_call(
        functools.partial(kernel, (days, steps, windows, width)),
        out_shape=jax.ShapeDtypeStruct((2, 2, steps, 2, width, width), f32),
        in_specs=[pl.BlockSpec(memory_space=pl.ANY), pl.BlockSpec(memory_space=pltpu.VMEM)],
        out_specs=pl.BlockSpec(memory_space=pl.ANY),
        scratch_shapes=[
            pltpu.VMEM((2, days, 2, steps, windows, width), bf16),
            pltpu.VMEM((2, steps, 2, days, windows, width), bf16),
            pltpu.VMEM((windows, width), f32),
            pltpu.VMEM((2, windows, width), f32),
            pltpu.VMEM((steps, days, 4, width, width), bf16),
            pltpu.VMEM((steps, days, 4, width, width), bf16),
            pltpu.VMEM((steps, 6, width, width), bf16),
            pltpu.VMEM((steps, 6, width, width), bf16),
            pltpu.VMEM((2, 2, steps, 2, width, width), f32),
            pltpu.VMEM((8, width), f32),
            pltpu.VMEM((days, 8, width), f32),
            pltpu.VMEM((8, width), f32),
            dma((days,)),
            dma((2, steps)),
            dma((2, steps)),
            dma((2,)),
            dma((2,)),
            dma((days,)),
            dma((days,)),
            dma((steps, days)),
            dma((steps, days)),
            dma((2, steps)),
            dma((2, steps)),
            dma((3, steps)),
        ],
        compiler_params=pltpu.CompilerParams(
            collective_id=0, has_side_effects=True, vmem_limit_bytes=60 * 1024 * 1024
        ),
        cost_estimate=pl.CostEstimate(flops=6_500_000_000, bytes_accessed=40_000_000, transcendentals=0),
    )(spectra.reshape(2, days, 2, steps, windows, width), marks)
    return stacked.reshape(2, 2 * steps, 2, width, width)


def solution(mesh):
    return jax.shard_map(
        per_device,
        mesh=mesh,
        in_specs=(P(None, None, "day", "block"), P("day", "block")),
        out_specs=P(None, "day", None, "block", None),
        check_vma=False,
    )
```

time: 836 us -> 185 us (0.22)
  waiting for transfers between devices: 601 us -> 0 us
  Pallas kernels: 0 us -> 179 us
  other arithmetic: 70.2 us -> 0.68 us
  local copies, waits for them, and re-layouts: 71.8 us -> 5.43 us
  matrix products: 40.5 us -> 0 us
  blocking collectives: 21.2 us -> 0 us
  between operations: 14.9 us -> 0.01 us
  starting transfers between devices: 9.07 us -> 0 us
    ppermute x4 -> x0, waiting for transfers between devices: 537 us -> none  [swapped(): return lax.ppermute(block, axis, route)]
    pallas_call x0 -> x1, Pallas kernels: none -> 179 us  [per_device(): pl.pallas_call(functools.partial(kernel, (days, steps, windows, width)),...]
    unnamed x4 -> x0, waiting for transfers between devices: 64 us -> none
    unnamed x10 -> x1, local copies, waits for them, and re-layouts: 50.9 us -> 4.7 us
    dot_general x2 -> x0, matrix products: 40.5 us -> none  [cross_terms(): jnp.einsum('fdwc,fdwe->dfce', left, right, preferred_element_type=jnp.flo...]
    another operation x4 -> x0, other arithmetic: 39.8 us -> none  [the longest x2 38.7 us: cross_terms(): return jnp.stack((real_part, imag_part), axis=2)]
    convert_element_type x6 -> x1, other arithmetic: 27.8 us -> 0.68 us  [per_device(): marks = jnp.broadcast_to(valid.astype(f32), (windows, width))]
    psum x1 -> x0, blocking collectives: 21.2 us -> none  [per_device(): shared = lax.psum(correlation, 'day')]
  transfers between devices with their start and end apart: 6 -> 0, of which waited for: 5 -> 0; matrix products, arithmetic and copies ran while one was open for 11% -> 0% of each run, Pallas kernels for 0% -> 0%
where the time goes in v1:
time: 185 us
  Pallas kernels  179 us (97%)
  local copies, waits for them, and re-layouts  5.43 us (3%)
    pallas_call x1, Pallas kernels, per_device(): pl.pallas_call(functools.partial(kernel, (days, steps, windows, width)),...  179 us
    unnamed x1, local copies, waits for them, and re-layouts  4.7 us

profile of v1, /device:TPU:0, one launch (start us, length us, event | category | flops | bytes accessed | tf_op | source)
XLA Modules:
  0.0 185.0 jit_solution(8763110454957872719)
XLA Ops:
  0.0 0.7 convert_element_type.3
  0.7 0.7 broadcast_in_dim.8.marks
  1.4 178.8 %shard_map.28 = f32[2,2,8,2,128,128]{5,4,3,2,1,0:T(8,128)} custom-call(bf16[2,8,2,8,192,128]{5,4,3,2,1,0:T(8,128)(2,1)} %bitcast.5, f32[192,128]{1,0:T(8,128)} %broadcast_in_dim.8.marks), custom_call_target="tpu_custom_call" | custom-call | flops 6499999744 | bytes 40000000 | tf_op jit(solution)/shard_map/pallas_call | solution.py:269
  180.3 4.7 %copy.4 = f32[2,16,2,128,128]{4,3,2,1,0:T(8,128)} copy(f32[2,16,2,128,128]{4,3,2,1,0:T(8,128)} %bitcast.3) | data formatting | bytes 8388608

commit v2 on v1

v2 whole, which is shorter than its diff:
```python
import functools

import jax
import jax.numpy as jnp
from jax import lax
from jax.experimental import pallas as pl
from jax.experimental.pallas import tpu as pltpu
from jax.sharding import PartitionSpec as P

EPSILON = 1e-06
RING = 4
AHEAD = 16
LATE = 3
VMEM_BYTES = 48 * 1024 * 1024
MESH = pl.DeviceIdType.MESH


def kernel(
    sizes, spectra, valid, out,
    own, taken, scale, scales_in, partial, partials_in, back, counts, counts_in, inverse,
    own_sem, row_send, row_recv, scale_send, scale_recv, count_send, count_recv,
    part_send, part_recv, back_send, back_recv,
):
    days, steps, windows, width = sizes
    units, early = days * steps, max(steps - LATE, 0)
    f32, bf16 = jnp.float32, jnp.bfloat16
    block, day = lax.axis_index("block"), lax.axis_index("day")
    rest_total = lax.axis_size("block") // RING
    row, rest = block // rest_total, block % rest_total
    row_q = row + 1 - 2 * (row % 2)
    row_r = RING - 1 - row
    peers = (row_q * rest_total + rest, row_r * rest_total + rest)
    mine = ((row + 1) // 2) % 2
    other = 1 - mine

    def owner(offset):
        return (day + offset) % days

    def row_copy(side, unit):
        half = other if side == 0 else mine
        step, index = unit // days, owner(unit + 1)
        return pltpu.make_async_remote_copy(
            src_ref=spectra.at[:, index, half, step],
            dst_ref=taken.at[side, step, :, index],
            send_sem=row_send.at[side, unit % AHEAD],
            recv_sem=row_recv.at[side, unit],
            device_id={"block": peers[side]},
            device_id_type=MESH,
        )

    def scale_copy(side):
        return pltpu.make_async_remote_copy(
            src_ref=scale,
            dst_ref=scales_in.at[side],
            send_sem=scale_send.at[side],
            recv_sem=scale_recv.at[side],
            device_id={"block": peers[side]},
            device_id_type=MESH,
        )

    def count_copy(offset):
        return pltpu.make_async_remote_copy(
            src_ref=counts,
            dst_ref=counts_in.at[offset],
            send_sem=count_send.at[offset],
            recv_sem=count_recv.at[offset],
            device_id={"day": owner(offset)},
            device_id_type=MESH,
        )

    def part_copy(step, offset):
        return pltpu.make_async_remote_copy(
            src_ref=partial.at[step, offset],
            dst_ref=partials_in.at[step, offset],
            send_sem=part_send.at[step, offset],
            recv_sem=part_recv.at[step, offset],
            device_id={"day": owner(offset)},
            device_id_type=MESH,
        )

    def back_copy(side, step):
        return pltpu.make_async_remote_copy(
            src_ref=back.at[step, pl.ds(0, 2)] if side == 0 else back.at[step, 2],
            dst_ref=out.at[:, mine, step] if side == 0 else out.at[0, mine, step],
            send_sem=back_send.at[side, step],
            recv_sem=back_recv.at[side, step],
            device_id={"block": peers[side]},
            device_id_type=MESH,
        )

    def back_wait(side, step):
        landed = out.at[:, other, step] if side == 0 else out.at[0, mine, step]
        pltpu.make_async_copy(landed, landed, back_recv.at[side, step]).wait()

    def own_copy(index):
        return pltpu.make_async_copy(spectra.at[:, index], own.at[:, index], own_sem.at[index])

    for index in range(days):
        own_copy(index).start()

    barrier = pltpu.get_barrier_semaphore()
    for side in range(2):
        pl.semaphore_signal(barrier, inc=1, device_id={"block": peers[side]}, device_id_type=MESH)
    for offset in range(1, days):
        pl.semaphore_signal(barrier, inc=1, device_id={"day": owner(offset)}, device_id_type=MESH)
    pl.semaphore_wait(barrier, days + 1)

    @pl.loop(0, AHEAD // 2)
    def _(unit):
        for side in range(2):
            row_copy(side, unit).start()

    tile = 48 if windows % 48 == 0 else 16
    scale[...] = jnp.zeros_like(scale)

    @pl.loop(0, days)
    def _(index):
        own_copy(index).wait()

        @pl.loop(0, windows // tile)
        def _(piece):
            rows = pl.ds(pl.multiple_of(piece * tile, tile), tile)
            total = scale[rows, :]
            for half in range(2):
                for step in range(steps):
                    for k in range(2):
                        value = own[k, index, half, step, rows, :].astype(f32)
                        total = total + value * value
            scale[rows, :] = total

    bins = days * 2 * steps
    marks = jnp.broadcast_to(valid[...].astype(f32), (width, windows)).T
    scale[...] = lax.rsqrt(scale[...] * (1.0 / bins) + EPSILON) * marks
    for side in range(2):
        scale_copy(side).start()

    @pl.loop(AHEAD // 2, AHEAD)
    def _(unit):
        for side in range(2):
            row_copy(side, unit).start()

    def whiten(value, factor):
        return (value.astype(f32) * factor).astype(bf16)

    def cross(step):
        @pl.loop(1, days + 1)
        def _(turn):
            offset = turn % days
            index = owner(offset)
            unit = step * days + turn - 1
            for side in range(2):
                row_copy(side, unit).wait_recv()
            parts = []
            for k in range(2):
                parts.append((
                    whiten(taken[0, step, k, index], scales_in[0]),
                    whiten(taken[1, step, k, index], scales_in[1]),
                    whiten(own[k, index, mine, step], scale[...]),
                ))
            (q_re, r_re, s_re), (q_im, r_im, s_im) = parts
            top = jnp.concatenate((r_re, r_im, s_re, s_im), axis=1)
            low = jnp.concatenate((r_im, -r_re, s_im, -s_re), axis=1)
            dims = (((0,), (0,)), ((), ()))
            gram = lax.dot_general(q_re, top, dims, preferred_element_type=f32)
            gram = gram + lax.dot_general(q_im, low, dims, preferred_element_type=f32)
            for part in range(4):
                partial[step, offset, part] = gram[:, part * width:(part + 1) * width].astype(bf16)

            @pl.when(offset != 0)
            def _():
                part_copy(step, offset).start()

            @pl.when(unit + AHEAD < units)
            def _():
                for side in range(2):
                    row_copy(side, unit).wait_send()
                    row_copy(side, unit + AHEAD).start()

    def reduce(step):
        @pl.loop(1, days)
        def _(offset):
            part_copy(step, offset).wait_recv()

        def total(part):
            value = partial[step, 0, part].astype(f32)
            for offset in range(1, days):
                value = value + partials_in[step, offset, part].astype(f32)
            return value * inverse[pl.ds(part // 2, 1), :]

        re0, im0, re1, im1 = total(0), total(1), total(2), total(3)
        back[step, 0, 0] = re0.astype(bf16)
        back[step, 0, 1] = im0.astype(bf16)
        back[step, 1, 0] = re1.astype(bf16)
        back[step, 1, 1] = im1.astype(bf16)
        back[step, 2, 0] = re0.T.astype(bf16)
        back[step, 2, 1] = (-im0.T).astype(bf16)

        @pl.when(jnp.logical_or(step < early, step == steps - 1))
        def _():
            for side in range(2):
                back_copy(side, step).start()

        out[1, mine, step, 0] = re1.T.astype(bf16)
        out[1, mine, step, 1] = (-im1.T).astype(bf16)

    for side in range(2):
        scale_copy(side).wait_recv()
    seen_q = jnp.where(scales_in[0] > 0, 1.0, 0.0)
    seen_r = jnp.where(scales_in[1] > 0, 1.0, 0.0)
    seen = jnp.where(scale[...] > 0, 1.0, 0.0)
    first = jnp.sum(seen_q * seen_r, axis=0, keepdims=True)
    second = jnp.sum(seen_q * seen, axis=0, keepdims=True)
    counts[...] = jnp.concatenate((first, second) * 4, axis=0)

    @pl.loop(1, days)
    def _(offset):
        count_copy(offset).start()

    @pl.loop(0, steps + 1)
    def _(turn):
        @pl.when(turn < steps)
        def _():
            cross(turn)

        @pl.when(turn == 1)
        def _():
            value = counts[...]
            for offset in range(1, days):
                count_copy(offset).wait_recv()
                value = value + counts_in[offset]
            inverse[...] = lax.rsqrt(value)

        @pl.when(turn == steps)
        def _():
            @pl.loop(early, steps - 1)
            def _(step):
                for side in range(2):
                    back_copy(side, step).start()

        @pl.when(turn >= 1)
        def _():
            reduce(turn - 1)

    @pl.loop(units - AHEAD, units)
    def _(unit):
        for side in range(2):
            row_copy(side, unit).wait_send()

    for side in range(2):
        scale_copy(side).wait_send()

    @pl.loop(1, days)
    def _(offset):
        count_copy(offset).wait_send()

    @pl.loop(0, steps)
    def _(step):
        @pl.loop(1, days)
        def _(offset):
            part_copy(step, offset).wait_send()

        for side in range(2):
            back_copy(side, step).wait_send()
            back_wait(side, step)


def per_device(spectra, valid):
    days = lax.axis_size("day")
    _, bins, windows, width = spectra.shape
    steps = bins // days // 2
    f32, bf16 = jnp.float32, jnp.bfloat16
    dma = pltpu.SemaphoreType.DMA
    stacked = pl.pallas_call(
        functools.partial(kernel, (days, steps, windows, width)),
        out_shape=pltpu.VMEM((2, 2, steps, 2, width, width), bf16),
        in_specs=[pl.BlockSpec(memory_space=pl.ANY), pl.BlockSpec(memory_space=pltpu.VMEM)],
        out_specs=pl.BlockSpec(memory_space=pltpu.VMEM),
        scratch_shapes=[
            pltpu.VMEM((2, days, 2, steps, windows, width), bf16),
            pltpu.VMEM((2, steps, 2, days, windows, width), bf16),
            pltpu.VMEM((windows, width), f32),
            pltpu.VMEM((2, windows, width), f32),
            pltpu.VMEM((steps, days, 4, width, width), bf16),
            pltpu.VMEM((steps, days, 4, width, width), bf16),
            pltpu.VMEM((steps, 3, 2, width, width), bf16),
            pltpu.VMEM((8, width), f32),
            pltpu.VMEM((days, 8, width), f32),
            pltpu.VMEM((8, width), f32),
            dma((days,)),
            dma((2, AHEAD)),
            dma((2, days * steps)),
            dma((2,)),
            dma((2,)),
            dma((days,)),
            dma((days,)),
            dma((steps, days)),
            dma((steps, days)),
            dma((2, steps)),
            dma((2, steps)),
        ],
        compiler_params=pltpu.CompilerParams(
            collective_id=0, has_side_effects=True, vmem_limit_bytes=VMEM_BYTES
        ),
        cost_estimate=pl.CostEstimate(flops=6_500_000_000, bytes_accessed=40_000_000, transcendentals=0),
    )(spectra.reshape(2, days, 2, steps, windows, width), valid.reshape(1, windows))
    return stacked.reshape(2, 2 * steps, 2, width, width).astype(f32)


def solution(mesh):
    return jax.shard_map(
        per_device,
        mesh=mesh,
        in_specs=(P(None, None, "day", "block"), P("day", "block")),
        out_specs=P(None, "day", None, "block", None),
        check_vma=False,
    )
```

time: 185 us -> 173 us (0.935)
  Pallas kernels: 179 us -> 169 us
  local copies, waits for them, and re-layouts: 5.43 us -> 0.68 us
  other arithmetic: 0.68 us -> 2.57 us
    pallas_call x1, Pallas kernels: 179 us -> 169 us  [per_device(): pl.pallas_call(functools.partial(kernel, (days, steps, windows, width)),...]
    unnamed x1 -> x2, local copies, waits for them, and re-layouts: 4.7 us -> 0.68 us
    convert_element_type x1, other arithmetic: 0.68 us -> 2.57 us  [per_device(): return stacked.reshape(2, 2 * steps, 2, width, width).astype(f32)]
where the time goes in v2:
time: 173 us; the launch traced here: 172 us
  Pallas kernels  169 us (98%)
  other arithmetic  2.57 us (1%)
    pallas_call x1, Pallas kernels, per_device(): pl.pallas_call(functools.partial(kernel, (days, steps, windows, width)),...  169 us

profile of v2, /device:TPU:0, one launch (start us, length us, event | category | flops | bytes accessed | tf_op | source)
XLA Modules:
  0.0 172.4 jit_solution(8102063985973219974)
XLA Ops:
  0.0 0.0 copy-start
  0.0 0.7 copy-done
  0.7 169.2 %shard_map.28 = bf16[2,2,8,2,128,128]{5,4,3,2,1,0:T(8,128)(2,1)S(1)} custom-call(bf16[2,8,2,8,192,128]{5,4,3,2,1,0:T(8,128)(2,1)} %bitcast.6, s32[1,192]{1,0:T(1,128)S(1)} %bitcast.5), custom_call_target="tpu_custom_call" | custom-call | flops 6499999744 | bytes 40000000 | tf_op jit(solution)/shard_map/pallas_call | solution.py:273
  169.9 2.6 %convert.1 = f32[2,16,2,128,128]{4,3,2,1,0:T(8,128)} convert(bf16[2,16,2,128,128]{4,3,2,1,0:T(8,128)(2,1)S(1)} %bitcast.4) | non-fusion elementwise | flops 1048576 | bytes 6291456 | tf_op jit(solution)/shard_map/convert_element_type | solution.py:306
Async XLA Ops:
  0.0 0.7 copy-start

commit v3 on v2

--- a/solution.py
+++ b/solution.py
@@ -9,7 +9,6 @@
 
 EPSILON = 1e-06
 RING = 4
-AHEAD = 16
 LATE = 3
 VMEM_BYTES = 48 * 1024 * 1024
 MESH = pl.DeviceIdType.MESH
@@ -17,12 +16,12 @@
 
 def kernel(
     sizes, spectra, valid, out,
-    own, taken, scale, scales_in, partial, partials_in, back, counts, counts_in, inverse,
-    own_sem, row_send, row_recv, scale_send, scale_recv, count_send, count_recv,
+    own, taken, scale, scale_out, scales_in, partial, partials_in, back, counts, counts_in, inverse,
+    seen_row, arrived, valid_sem, own_sem, row_send, row_recv, scale_send, scale_recv, count_send, count_recv,
     part_send, part_recv, back_send, back_recv,
 ):
     days, steps, windows, width = sizes
-    units, early = days * steps, max(steps - LATE, 0)
+    last, early = steps - 1, steps - LATE
     f32, bf16 = jnp.float32, jnp.bfloat16
     block, day = lax.axis_index("block"), lax.axis_index("day")
     rest_total = lax.axis_size("block") // RING
@@ -33,24 +32,30 @@
     mine = ((row + 1) // 2) % 2
     other = 1 - mine
 
+    along, across = day % RING, day // RING
+    nearest = [across * RING + (along + 1) % RING, across * RING + (along + RING - 1) % RING]
+    if days > RING:
+        nearest.append((1 - across) * RING + along)
+
     def owner(offset):
         return (day + offset) % days
 
-    def row_copy(side, unit):
+    def row_copy(side, step, index=None):
         half = other if side == 0 else mine
-        step, index = unit // days, owner(unit + 1)
+        slot = step if index is None else last + index
+        index = slice(None) if index is None else index
         return pltpu.make_async_remote_copy(
             src_ref=spectra.at[:, index, half, step],
             dst_ref=taken.at[side, step, :, index],
-            send_sem=row_send.at[side, unit % AHEAD],
-            recv_sem=row_recv.at[side, unit],
+            send_sem=row_send.at[side, slot],
+            recv_sem=row_recv.at[side, slot],
             device_id={"block": peers[side]},
             device_id_type=MESH,
         )
 
     def scale_copy(side):
         return pltpu.make_async_remote_copy(
-            src_ref=scale,
+            src_ref=scale_out,
             dst_ref=scales_in.at[side],
             send_sem=scale_send.at[side],
             recv_sem=scale_recv.at[side],
@@ -95,20 +100,25 @@
     def own_copy(index):
         return pltpu.make_async_copy(spectra.at[:, index], own.at[:, index], own_sem.at[index])
 
+    valid_copy = pltpu.make_async_copy(valid, seen_row, valid_sem)
+    valid_copy.start()
     for index in range(days):
         own_copy(index).start()
 
     barrier = pltpu.get_barrier_semaphore()
     for side in range(2):
         pl.semaphore_signal(barrier, inc=1, device_id={"block": peers[side]}, device_id_type=MESH)
-    for offset in range(1, days):
-        pl.semaphore_signal(barrier, inc=1, device_id={"day": owner(offset)}, device_id_type=MESH)
-    pl.semaphore_wait(barrier, days + 1)
-
-    @pl.loop(0, AHEAD // 2)
-    def _(unit):
-        for side in range(2):
-            row_copy(side, unit).start()
+    for near in nearest:
+        pl.semaphore_signal(barrier, inc=1, device_id={"day": near}, device_id_type=MESH)
+    pl.semaphore_wait(barrier, 2 + len(nearest))
+
+    for side in range(2):
+        row_copy(side, 0).start()
+
+    for hop in range(2):
+        for near in nearest:
+            pl.semaphore_signal(arrived.at[hop], inc=1, device_id={"day": near}, device_id_type=MESH)
+        pl.semaphore_wait(arrived.at[hop], len(nearest))
 
     tile = 48 if windows % 48 == 0 else 16
     scale[...] = jnp.zeros_like(scale)
@@ -129,32 +139,52 @@
             scale[rows, :] = total
 
     bins = days * 2 * steps
-    marks = jnp.broadcast_to(valid[...].astype(f32), (width, windows)).T
+    valid_copy.wait()
+    marks = jnp.broadcast_to(seen_row[...].astype(f32), (width, windows)).T
     scale[...] = lax.rsqrt(scale[...] * (1.0 / bins) + EPSILON) * marks
+    scale_out[...] = scale[...].astype(bf16)
     for side in range(2):
         scale_copy(side).start()
 
-    @pl.loop(AHEAD // 2, AHEAD)
-    def _(unit):
-        for side in range(2):
-            row_copy(side, unit).start()
+    for side in range(2):
+        row_copy(side, 1).start()
 
     def whiten(value, factor):
         return (value.astype(f32) * factor).astype(bf16)
 
     def cross(step):
+        @pl.when(step < last)
+        def _():
+            for side in range(2):
+                row_copy(side, step).wait_recv()
+                row_copy(side, step).wait_send()
+
+                @pl.when(step + 2 < last)
+                def _():
+                    row_copy(side, step + 2).start()
+
+        @pl.when(step + 2 == last)
+        def _():
+            @pl.loop(1, days + 1)
+            def _(turn):
+                for side in range(2):
+                    row_copy(side, last, owner(turn)).start()
+
         @pl.loop(1, days + 1)
         def _(turn):
             offset = turn % days
             index = owner(offset)
-            unit = step * days + turn - 1
-            for side in range(2):
-                row_copy(side, unit).wait_recv()
+
+            @pl.when(step == last)
+            def _():
+                for side in range(2):
+                    row_copy(side, last, index).wait_recv()
+
             parts = []
             for k in range(2):
                 parts.append((
-                    whiten(taken[0, step, k, index], scales_in[0]),
-                    whiten(taken[1, step, k, index], scales_in[1]),
+                    whiten(taken[0, step, k, index], scales_in[0].astype(f32)),
+                    whiten(taken[1, step, k, index], scales_in[1].astype(f32)),
                     whiten(own[k, index, mine, step], scale[...]),
                 ))
             (q_re, r_re, s_re), (q_im, r_im, s_im) = parts
@@ -170,12 +200,6 @@
             def _():
                 part_copy(step, offset).start()
 
-            @pl.when(unit + AHEAD < units)
-            def _():
-                for side in range(2):
-                    row_copy(side, unit).wait_send()
-                    row_copy(side, unit + AHEAD).start()
-
     def reduce(step):
         @pl.loop(1, days)
         def _(offset):
@@ -241,10 +265,10 @@
         def _():
             reduce(turn - 1)
 
-    @pl.loop(units - AHEAD, units)
-    def _(unit):
+    @pl.loop(0, days)
+    def _(index):
         for side in range(2):
-            row_copy(side, unit).wait_send()
+            row_copy(side, last, index).wait_send()
 
     for side in range(2):
         scale_copy(side).wait_send()
@@ -259,6 +283,8 @@
         def _(offset):
             part_copy(step, offset).wait_send()
 
+    @pl.loop(0, steps)
+    def _(step):
         for side in range(2):
             back_copy(side, step).wait_send()
             back_wait(side, step)
@@ -273,22 +299,26 @@
     stacked = pl.pallas_call(
         functools.partial(kernel, (days, steps, windows, width)),
         out_shape=pltpu.VMEM((2, 2, steps, 2, width, width), bf16),
-        in_specs=[pl.BlockSpec(memory_space=pl.ANY), pl.BlockSpec(memory_space=pltpu.VMEM)],
+        in_specs=[pl.BlockSpec(memory_space=pltpu.HBM)] * 2,
         out_specs=pl.BlockSpec(memory_space=pltpu.VMEM),
         scratch_shapes=[
             pltpu.VMEM((2, days, 2, steps, windows, width), bf16),
             pltpu.VMEM((2, steps, 2, days, windows, width), bf16),
             pltpu.VMEM((windows, width), f32),
-            pltpu.VMEM((2, windows, width), f32),
+            pltpu.VMEM((windows, width), bf16),
+            pltpu.VMEM((2, windows, width), bf16),
             pltpu.VMEM((steps, days, 4, width, width), bf16),
             pltpu.VMEM((steps, days, 4, width, width), bf16),
             pltpu.VMEM((steps, 3, 2, width, width), bf16),
             pltpu.VMEM((8, width), f32),
             pltpu.VMEM((days, 8, width), f32),
             pltpu.VMEM((8, width), f32),
+            pltpu.VMEM((1, windows), jnp.int32),
+            pltpu.SemaphoreType.REGULAR((2,)),
+            dma,
             dma((days,)),
-            dma((2, AHEAD)),
-            dma((2, days * steps)),
+            dma((2, steps - 1 + days)),
+            dma((2, steps - 1 + days)),
             dma((2,)),
             dma((2,)),
             dma((days,)),
@@ -302,7 +332,7 @@
             collective_id=0, has_side_effects=True, vmem_limit_bytes=VMEM_BYTES
         ),
         cost_estimate=pl.CostEstimate(flops=6_500_000_000, bytes_accessed=40_000_000, transcendentals=0),
-    )(spectra.reshape(2, days, 2, steps, windows, width), valid.reshape(1, windows))
+    )(spectra.reshape(2, days, 2, steps, windows, width), pltpu.with_memory_space_constraint(valid.reshape(1, windows), pltpu.HBM))
     return stacked.reshape(2, 2 * steps, 2, width, width).astype(f32)
 
 

time: 173 us -> 169 us (0.977)
  Pallas kernels: 169 us -> 166 us
    pallas_call x1, Pallas kernels: 169 us -> 166 us  [per_device(): pl.pallas_call(functools.partial(kernel, (days, steps, windows, width)),...]
where the time goes in v3:
time: 169 us; the launch traced here: 168 us
  Pallas kernels  166 us (98%)
  other arithmetic  2.54 us (2%)
    pallas_call x1, Pallas kernels, per_device(): pl.pallas_call(functools.partial(kernel, (days, steps, windows, width)),...  166 us

profile of v3, /device:TPU:0, one launch (start us, length us, event | category | flops | bytes accessed | tf_op | source)
XLA Modules:
  0.0 168.3 jit_solution(17612535519871665248)
XLA Ops:
  0.0 165.7 %shard_map.28 = bf16[2,2,8,2,128,128]{5,4,3,2,1,0:T(8,128)(2,1)S(1)} custom-call(bf16[2,8,2,8,192,128]{5,4,3,2,1,0:T(8,128)(2,1)} %bitcast.5, s32[1,192]{1,0:T(1,128)} %bitcast.6), custom_call_target="tpu_custom_call" | custom-call | flops 6499999744 | bytes 40000000 | tf_op jit(solution)/shard_map/pallas_call | solution.py:299
  165.7 2.5 %convert.1 = f32[2,16,2,128,128]{4,3,2,1,0:T(8,128)} convert(bf16[2,16,2,128,128]{4,3,2,1,0:T(8,128)(2,1)S(1)} %bitcast.4) | non-fusion elementwise | flops 1048576 | bytes 6291456 | tf_op jit(solution)/shard_map/convert_element_type | solution.py:336

commit v4 on v3

--- a/solution.py
+++ b/solution.py
@@ -9,7 +9,8 @@
 
 EPSILON = 1e-06
 RING = 4
-LATE = 3
+LATE = 2
+PIECES = 8
 VMEM_BYTES = 48 * 1024 * 1024
 MESH = pl.DeviceIdType.MESH
 
@@ -33,19 +34,24 @@
     other = 1 - mine
 
     along, across = day % RING, day // RING
-    nearest = [across * RING + (along + 1) % RING, across * RING + (along + RING - 1) % RING]
-    if days > RING:
-        nearest.append((1 - across) * RING + along)
+    place = along + across * (days - 1 - 2 * along)
+
+    def ringed(spot):
+        spot = spot % days
+        far = spot // RING
+        return far * RING + spot % RING + far * (RING - 1 - 2 * (spot % RING))
+
+    after, before = ringed(place + 1), ringed(place + days - 1)
 
     def owner(offset):
         return (day + offset) % days
 
-    def row_copy(side, step, index=None):
+    def row_copy(side, step, index=None, source=own):
         half = other if side == 0 else mine
         slot = step if index is None else last + index
         index = slice(None) if index is None else index
         return pltpu.make_async_remote_copy(
-            src_ref=spectra.at[:, index, half, step],
+            src_ref=source.at[:, index, half, step],
             dst_ref=taken.at[side, step, :, index],
             send_sem=row_send.at[side, slot],
             recv_sem=row_recv.at[side, slot],
@@ -108,17 +114,18 @@
     barrier = pltpu.get_barrier_semaphore()
     for side in range(2):
         pl.semaphore_signal(barrier, inc=1, device_id={"block": peers[side]}, device_id_type=MESH)
-    for near in nearest:
-        pl.semaphore_signal(barrier, inc=1, device_id={"day": near}, device_id_type=MESH)
-    pl.semaphore_wait(barrier, 2 + len(nearest))
-
-    for side in range(2):
-        row_copy(side, 0).start()
-
-    for hop in range(2):
-        for near in nearest:
+    pl.semaphore_signal(barrier, inc=1, device_id={"day": before}, device_id_type=MESH)
+    pl.semaphore_wait(barrier, 3)
+
+    for side in range(2):
+        row_copy(side, 0, source=spectra).start()
+
+    pl.semaphore_signal(arrived.at[0], inc=1, device_id={"day": after}, device_id_type=MESH)
+    pl.semaphore_wait(arrived.at[0], 1)
+    for hop in range(1, days // 2):
+        for near in (after, before):
             pl.semaphore_signal(arrived.at[hop], inc=1, device_id={"day": near}, device_id_type=MESH)
-        pl.semaphore_wait(arrived.at[hop], len(nearest))
+        pl.semaphore_wait(arrived.at[hop], 2)
 
     tile = 48 if windows % 48 == 0 else 16
     scale[...] = jnp.zeros_like(scale)
@@ -146,13 +153,28 @@
     for side in range(2):
         scale_copy(side).start()
 
-    for side in range(2):
-        row_copy(side, 1).start()
-
     def whiten(value, factor):
         return (value.astype(f32) * factor).astype(bf16)
 
+    def prepare(step):
+        factor = scale[...]
+
+        @pl.loop(0, days)
+        def _(index):
+            for half in range(2):
+                for k in range(2):
+                    own[k, index, half, step] = whiten(own[k, index, half, step], factor)
+
+    prepare(1)
+    for side in range(2):
+        row_copy(side, 1).start()
+    prepare(0)
+
     def cross(step):
+        @pl.when(step + 2 <= last)
+        def _():
+            prepare(step + 2)
+
         @pl.when(step < last)
         def _():
             for side in range(2):
@@ -180,14 +202,16 @@
                 for side in range(2):
                     row_copy(side, last, index).wait_recv()
 
-            parts = []
-            for k in range(2):
-                parts.append((
-                    whiten(taken[0, step, k, index], scales_in[0].astype(f32)),
-                    whiten(taken[1, step, k, index], scales_in[1].astype(f32)),
-                    whiten(own[k, index, mine, step], scale[...]),
-                ))
-            (q_re, r_re, s_re), (q_im, r_im, s_im) = parts
+            @pl.when(step == 0)
+            def _():
+                for side in range(2):
+                    factor = scales_in[side].astype(f32)
+                    for k in range(2):
+                        taken[side, 0, k, index] = whiten(taken[side, 0, k, index], factor)
+
+            q_re, q_im = taken[0, step, 0, index], taken[0, step, 1, index]
+            r_re, r_im = taken[1, step, 0, index], taken[1, step, 1, index]
+            s_re, s_im = own[0, index, mine, step], own[1, index, mine, step]
             top = jnp.concatenate((r_re, r_im, s_re, s_im), axis=1)
             low = jnp.concatenate((r_im, -r_re, s_im, -s_re), axis=1)
             dims = (((0,), (0,)), ((), ()))
@@ -288,6 +312,19 @@
         for side in range(2):
             back_copy(side, step).wait_send()
             back_wait(side, step)
+
+
+def widen(narrow, wide, staged, sem):
+    pieces = narrow.shape[0]
+
+    def piece_copy(piece):
+        return pltpu.make_async_copy(staged.at[piece], wide.at[piece], sem.at[piece])
+
+    for piece in range(pieces):
+        staged[piece] = narrow[piece].astype(jnp.float32)
+        piece_copy(piece).start()
+    for piece in range(pieces):
+        piece_copy(piece).wait()
 
 
 def per_device(spectra, valid):
@@ -314,7 +351,7 @@
             pltpu.VMEM((days, 8, width), f32),
             pltpu.VMEM((8, width), f32),
             pltpu.VMEM((1, windows), jnp.int32),
-            pltpu.SemaphoreType.REGULAR((2,)),
+            pltpu.SemaphoreType.REGULAR((days // 2,)),
             dma,
             dma((days,)),
             dma((2, steps - 1 + days)),
@@ -333,7 +370,16 @@
         ),
         cost_estimate=pl.CostEstimate(flops=6_500_000_000, bytes_accessed=40_000_000, transcendentals=0),
     )(spectra.reshape(2, days, 2, steps, windows, width), pltpu.with_memory_space_constraint(valid.reshape(1, windows), pltpu.HBM))
-    return stacked.reshape(2, 2 * steps, 2, width, width).astype(f32)
+    pieces = (PIECES, 8 * steps * width // PIECES, width)
+    stacked = pl.pallas_call(
+        widen,
+        out_shape=jax.ShapeDtypeStruct(pieces, f32),
+        in_specs=[pl.BlockSpec(memory_space=pltpu.VMEM)],
+        out_specs=pl.BlockSpec(memory_space=pl.ANY),
+        scratch_shapes=[pltpu.VMEM(pieces, f32), dma((PIECES,))],
+        compiler_params=pltpu.CompilerParams(vmem_limit_bytes=16 * 1024 * 1024),
+    )(stacked.reshape(pieces))
+    return stacked.reshape(2, 2 * steps, 2, width, width)
 
 
 def solution(mesh):

time: 169 us -> 167 us (0.988)
  other arithmetic: 2.54 us -> 0 us
    convert_element_type x1 -> x0, other arithmetic: 2.54 us -> none  [per_device(): return stacked.reshape(2, 2 * steps, 2, width, width).astype(f32)]
    pallas_call x0 -> x1, Pallas kernels: none -> 2.11 us  [per_device(): pl.pallas_call(widen, out_shape=jax.ShapeDtypeStruct(pieces, f32), in_spe...]
where the time goes in v4:
time: 167 us
  Pallas kernels  167 us (100%)
    pallas_call x1, Pallas kernels, per_device(): pl.pallas_call(functools.partial(kernel, (days, steps, windows, width)),...  165 us

profile of v4, /device:TPU:0, one launch (start us, length us, event | category | flops | bytes accessed | tf_op | source)
XLA Modules:
  0.0 166.8 jit_solution(685474372935886979)
XLA Ops:
  0.0 164.7 %shard_map.28 = bf16[2,2,8,2,128,128]{5,4,3,2,1,0:T(8,128)(2,1)S(1)} custom-call(bf16[2,8,2,8,192,128]{5,4,3,2,1,0:T(8,128)(2,1)} %bitcast.5, s32[1,192]{1,0:T(1,128)} %bitcast.6), custom_call_target="tpu_custom_call" | custom-call | flops 6499999744 | bytes 40000000 | tf_op jit(solution)/shard_map/pallas_call | solution.py:336
  164.7 2.1 %shard_map.29 = f32[8,1024,128]{2,1,0:T(8,128)} custom-call(bf16[8,1024,128]{2,1,0:T(8,128)(2,1)S(1)} %bitcast.4), custom_call_target="tpu_custom_call" | custom-call | tf_op jit(solution)/shard_map/pallas_call | solution.py:374

commit v5 on v4

--- a/solution.py
+++ b/solution.py
@@ -10,14 +10,15 @@
 EPSILON = 1e-06
 RING = 4
 LATE = 2
+GAP = 1
 PIECES = 8
 VMEM_BYTES = 48 * 1024 * 1024
 MESH = pl.DeviceIdType.MESH
 
 
 def kernel(
-    sizes, spectra, valid, out,
-    own, taken, scale, scale_out, scales_in, partial, partials_in, back, counts, counts_in, inverse,
+    sizes, spectra, valid, result,
+    out, own, taken, scale, scale_out, scales_in, partial, partials_in, back, counts, counts_in, inverse,
     seen_row, arrived, valid_sem, own_sem, row_send, row_recv, scale_send, scale_recv, count_send, count_recv,
     part_send, part_recv, back_send, back_recv,
 ):
@@ -170,6 +171,33 @@
         row_copy(side, 1).start()
     prepare(0)
 
+    def reduce(step):
+        @pl.loop(1, days)
+        def _(offset):
+            part_copy(step, offset).wait_recv()
+
+        def total(part):
+            value = partial[step, 0, part].astype(f32)
+            for offset in range(1, days):
+                value = value + partials_in[step, offset, part].astype(f32)
+            return value * inverse[pl.ds(part // 2, 1), :]
+
+        re0, im0, re1, im1 = total(0), total(1), total(2), total(3)
+        back[step, 0, 0] = re0.astype(bf16)
+        back[step, 0, 1] = im0.astype(bf16)
+        back[step, 1, 0] = re1.astype(bf16)
+        back[step, 1, 1] = im1.astype(bf16)
+        back[step, 2, 0] = re0.T.astype(bf16)
+        back[step, 2, 1] = (-im0.T).astype(bf16)
+
+        @pl.when(jnp.logical_or(step < early, step == steps - 1))
+        def _():
+            for side in range(2):
+                back_copy(side, step).start()
+
+        out[1, mine, step, 0] = re1.T.astype(bf16)
+        out[1, mine, step, 1] = (-im1.T).astype(bf16)
+
     def cross(step):
         @pl.when(step + 2 <= last)
         def _():
@@ -224,32 +252,9 @@
             def _():
                 part_copy(step, offset).start()
 
-    def reduce(step):
-        @pl.loop(1, days)
-        def _(offset):
-            part_copy(step, offset).wait_recv()
-
-        def total(part):
-            value = partial[step, 0, part].astype(f32)
-            for offset in range(1, days):
-                value = value + partials_in[step, offset, part].astype(f32)
-            return value * inverse[pl.ds(part // 2, 1), :]
-
-        re0, im0, re1, im1 = total(0), total(1), total(2), total(3)
-        back[step, 0, 0] = re0.astype(bf16)
-        back[step, 0, 1] = im0.astype(bf16)
-        back[step, 1, 0] = re1.astype(bf16)
-        back[step, 1, 1] = im1.astype(bf16)
-        back[step, 2, 0] = re0.T.astype(bf16)
-        back[step, 2, 1] = (-im0.T).astype(bf16)
-
-        @pl.when(jnp.logical_or(step < early, step == steps - 1))
-        def _():
-            for side in range(2):
-                back_copy(side, step).start()
-
-        out[1, mine, step, 0] = re1.T.astype(bf16)
-        out[1, mine, step, 1] = (-im1.T).astype(bf16)
+            @pl.when(jnp.logical_and(turn == days - GAP, step == last))
+            def _():
+                reduce(step - 1)
 
     for side in range(2):
         scale_copy(side).wait_recv()
@@ -285,7 +290,7 @@
                 for side in range(2):
                     back_copy(side, step).start()
 
-        @pl.when(turn >= 1)
+        @pl.when(jnp.logical_and(turn >= 1, turn != last))
         def _():
             reduce(turn - 1)
 
@@ -312,18 +317,16 @@
         for side in range(2):
             back_copy(side, step).wait_send()
             back_wait(side, step)
-
-
-def widen(narrow, wide, staged, sem):
-    pieces = narrow.shape[0]
-
+        result[:, :, step] = out[:, :, step].astype(f32)
+
+
+def store(held, stored, sem):
     def piece_copy(piece):
-        return pltpu.make_async_copy(staged.at[piece], wide.at[piece], sem.at[piece])
-
-    for piece in range(pieces):
-        staged[piece] = narrow[piece].astype(jnp.float32)
+        return pltpu.make_async_copy(held.at[piece], stored.at[piece], sem.at[piece])
+
+    for piece in range(PIECES):
         piece_copy(piece).start()
-    for piece in range(pieces):
+    for piece in range(PIECES):
         piece_copy(piece).wait()
 
 
@@ -335,10 +338,11 @@
     dma = pltpu.SemaphoreType.DMA
     stacked = pl.pallas_call(
         functools.partial(kernel, (days, steps, windows, width)),
-        out_shape=pltpu.VMEM((2, 2, steps, 2, width, width), bf16),
+        out_shape=pltpu.VMEM((2, 2, steps, 2, width, width), f32),
         in_specs=[pl.BlockSpec(memory_space=pltpu.HBM)] * 2,
         out_specs=pl.BlockSpec(memory_space=pltpu.VMEM),
         scratch_shapes=[
+            pltpu.VMEM((2, 2, steps, 2, width, width), bf16),
             pltpu.VMEM((2, days, 2, steps, windows, width), bf16),
             pltpu.VMEM((2, steps, 2, days, windows, width), bf16),
             pltpu.VMEM((windows, width), f32),
@@ -372,12 +376,12 @@
     )(spectra.reshape(2, days, 2, steps, windows, width), pltpu.with_memory_space_constraint(valid.reshape(1, windows), pltpu.HBM))
     pieces = (PIECES, 8 * steps * width // PIECES, width)
     stacked = pl.pallas_call(
-        widen,
+        store,
         out_shape=jax.ShapeDtypeStruct(pieces, f32),
         in_specs=[pl.BlockSpec(memory_space=pltpu.VMEM)],
         out_specs=pl.BlockSpec(memory_space=pl.ANY),
-        scratch_shapes=[pltpu.VMEM(pieces, f32), dma((PIECES,))],
-        compiler_params=pltpu.CompilerParams(vmem_limit_bytes=16 * 1024 * 1024),
+        scratch_shapes=[dma((PIECES,))],
+        compiler_params=pltpu.CompilerParams(vmem_limit_bytes=8 * 1024 * 1024),
     )(stacked.reshape(pieces))
     return stacked.reshape(2, 2 * steps, 2, width, width)
 

time: 167 us -> 167 us (level)
  no operation moved by 1% of the time
where the time goes in v5:
time: 167 us
  Pallas kernels  167 us (100%)
    pallas_call x1, Pallas kernels, per_device(): pl.pallas_call(functools.partial(kernel, (days, steps, windows, width)),...  165 us

profile of v5, /device:TPU:0, one launch (start us, length us, event | category | flops | bytes accessed | tf_op | source)
XLA Modules:
  0.0 166.8 jit_solution(2478035396938920751)
XLA Ops:
  0.0 164.7 %shard_map.28 = f32[2,2,8,2,128,128]{5,4,3,2,1,0:T(8,128)S(1)} custom-call(bf16[2,8,2,8,192,128]{5,4,3,2,1,0:T(8,128)(2,1)} %bitcast.5, s32[1,192]{1,0:T(1,128)} %bitcast.6), custom_call_target="tpu_custom_call" | custom-call | flops 6499999744 | bytes 40000000 | tf_op jit(solution)/shard_map/pallas_call | solution.py:339
  164.8 2.1 %shard_map.29 = f32[8,1024,128]{2,1,0:T(8,128)} custom-call(f32[8,1024,128]{2,1,0:T(8,128)S(1)} %bitcast.4), custom_call_target="tpu_custom_call" | custom-call | tf_op jit(solution)/shard_map/pallas_call | solution.py:378
